TPU v7x, 32 devices: a whole 2x2x4 slice. The times are simulated.
32 devices in a mesh: sub: 8 (over z, y), fac: 4 (over x, core).
Axes of the slice: x: 2, y: 2, z: 4, core: 2. Of those that a mesh axis runs over, the one named last changes fastest.
Arguments:
- visibility: bfloat16 [12288, 256], P(('sub', 'fac')), may hold values from -6 to 6
- vis_weight: bfloat16 [12288, 128], P(('sub', 'fac')), may hold values from 0.099609375 to 1
- tap_start: int32 [12288, 2], P(('sub', 'fac')), may hold values from 4096 to 127999
- tap_step: int32 [12288, 2], P(('sub', 'fac')), may hold values from 102 to 818
- subgrid_id: int32 [12288], P(('sub', 'fac')), may hold values from 0 to 23, as said below
- w_plane: int32 [12288], P(('sub', 'fac')), may hold values from 0 to 3
- tile_intersection: int32 [24, 2], P('sub'), may hold values from 0 to 7936, as said below
Outputs:
- uv_planes: float32 [4, 2, 1024, 8192], P('fac', None, 'sub')
Inputs may be any that keep to these rules, and one draw needn't show every extreme that they name: Within the rows of one device at most 8 rows name the same pair of subgrid_id and w_plane, and one pair is named by exactly 8 rows of every device. `tile_intersection`: column 0 is below 128; column 1 is at most 7936.
All inputs are finite; a program needn't handle non-finite values.
Results may differ from a plain program's by a relative error of at most 0.0038.
Values may be sent and summed in bfloat16 or wider, within the bound.
A program may use at most 64 MiB of HBM per device.

v0:
```python
import math

import jax
import jax.numpy as jnp
from jax import lax
from jax.sharding import PartitionSpec as P

SG = 256
GS = 8192
BAND = 128


kernel_beta = 18.0
kernel_norm = 1.6e-07
fixed_unit = 1.0 / 1024.0


def from_behind(block, axis, distance):
    devices = range(lax.axis_size(axis))
    route = [((i - distance) % len(devices), i) for i in devices]
    return lax.ppermute(block, axis, route)


def bessel_zero(value):
    quarter = value * value * 0.25
    term = jnp.ones_like(value)
    total = jnp.ones_like(value)
    for order in range(1, 40):
        term = term * quarter * (1.0 / (order * order))
        total = total + term
    return total


def kaiser(offset):
    inside = jnp.maximum(1.0 - offset * offset * 0.0625, 0.0)
    return (bessel_zero(kernel_beta * jnp.sqrt(inside)) - 1.0) * kernel_norm


def track_positions(track, chans):
    channel = jnp.arange(chans, dtype=jnp.int32)
    along_u = track[:, 0:1] + channel[None, :] * track[:, 2:3]
    along_v = track[:, 1:2] + channel[None, :] * track[:, 3:4]
    return (along_u.astype(jnp.float32) * fixed_unit, along_v.astype(jnp.float32) * fixed_unit)


def kernel_taps(position):
    start = jnp.floor(position) - 3.0
    spread = jnp.arange(8, dtype=jnp.float32)
    return (kaiser(start[..., None] + spread - position[..., None]), start)


def dense_kernel(weights, start, cells):
    offset = cells - start[..., None]
    result = jnp.zeros(offset.shape, jnp.float32)
    for tap in range(8):
        result = jnp.where(offset == tap, weights[..., tap : tap + 1], result)
    return result


def grid_rows(visible, weight, track, side):
    total, chans = weight.shape
    block = math.gcd(total, max(8, 2048 // chans))
    count = total // block
    cells = jnp.arange(side, dtype=jnp.float32)[None, None, :]

    def step(accum, pieces):
        vis_block, weight_block, track_block = pieces
        pos_u, pos_v = track_positions(track_block, chans)
        weights_u, start_u = kernel_taps(pos_u)
        weights_v, start_v = kernel_taps(pos_v)
        dense_u = dense_kernel(weights_u, start_u, cells)
        dense_v = dense_kernel(weights_v, start_v, cells)
        scaled = (
            vis_block.astype(jnp.float32).reshape(block, 2, chans)
            * weight_block.astype(jnp.float32)[:, None, :]
        )
        left = (jnp.transpose(scaled, (0, 2, 1))[..., None] * dense_v[:, :, None, :]).astype(
            jnp.bfloat16
        )
        left = left.reshape(block * chans, 2 * side)
        right = dense_u.astype(jnp.bfloat16).reshape(block * chans, side)
        added = lax.dot_general(
            left, right, (((0,), (0,)), ((), ())), preferred_element_type=jnp.float32
        )
        return (accum + added, None)

    pieces = (
        visible.reshape(count, block, 2 * chans),
        weight.reshape(count, block, chans),
        track.reshape(count, block, 4),
    )
    accum, unused = lax.scan(step, jnp.zeros((2 * side, side), jnp.float32), pieces)
    return accum.reshape(2, side, side)


def spread_rows(grid, first_row):
    zero = jnp.zeros((), jnp.int32)
    padded = jnp.zeros((2, 3 * BAND, SG), jnp.float32)
    return lax.dynamic_update_slice(padded, grid, (zero, first_row, zero))


def place_piece(band, piece, column):
    zero = jnp.zeros((), jnp.int32)
    current = lax.dynamic_slice(band, (zero, zero, column), (2, BAND, SG))
    return lax.dynamic_update_slice(band, current + piece, (zero, zero, column))


def shards(visibility, vis_weight, tap_start, tap_step, subgrid_id, w_plane, tile_intersection):
    sub_count = lax.axis_size("sub")
    fac_count = lax.axis_size("fac")
    rows, chans = vis_weight.shape
    local_grids = tile_intersection.shape[0]
    dest_count = sub_count * fac_count * local_grids
    capacity = max(2, (2 * rows + dest_count - 1) // dest_count)
    target = (
        subgrid_id // local_grids * fac_count + w_plane
    ) * local_grids + subgrid_id % local_grids
    onehot = (target[:, None] == jnp.arange(dest_count, dtype=jnp.int32)[None, :]).astype(jnp.int32)
    before = jnp.cumsum(onehot, axis=0) - onehot
    rank = jnp.sum(before * onehot, axis=1)
    slot = target * capacity + rank
    track = jnp.concatenate([tap_start, tap_step], axis=1)
    slot_total = dest_count * capacity
    send_vis = jnp.zeros((slot_total, 2 * chans), jnp.bfloat16).at[slot].set(visibility)
    send_weight = jnp.zeros((slot_total, chans), jnp.bfloat16).at[slot].set(vis_weight)
    send_track = jnp.zeros((slot_total, 4), jnp.int32).at[slot].set(track)
    leading = (sub_count * fac_count, local_grids, capacity)
    got_vis, got_weight, got_track = (
        lax.all_to_all(
            send_vis.reshape(leading + (2 * chans,)),
            ("sub", "fac"),
            split_axis=0,
            concat_axis=0,
            tiled=True,
        ),
        lax.all_to_all(
            send_weight.reshape(leading + (chans,)),
            ("sub", "fac"),
            split_axis=0,
            concat_axis=0,
            tiled=True,
        ),
        lax.all_to_all(
            send_track.reshape(leading + (4,)),
            ("sub", "fac"),
            split_axis=0,
            concat_axis=0,
            tiled=True,
        ),
    )
    grids = []
    for member in range(local_grids):
        grids.append(
            grid_rows(
                got_vis[:, member].reshape(-1, 2 * chans),
                got_weight[:, member].reshape(-1, chans),
                got_track[:, member].reshape(-1, 4),
                SG,
            )
        )
    stacked = jnp.stack(grids)
    pieces = jax.vmap(spread_rows)(stacked, tile_intersection[:, 0]).reshape(
        local_grids, 2, 3, BAND, SG
    )
    own_rows = pieces[:, :, 0]
    next_rows = pieces[:, :, 1]
    far_rows = pieces[:, :, 2]
    columns = tile_intersection[:, 1]
    got_next, next_cols = from_behind((next_rows, columns), "sub", 1)
    got_far, far_cols = from_behind((far_rows, columns), "sub", 2)
    band = jnp.zeros((2, BAND, GS), jnp.float32)
    for member in range(local_grids):
        band = place_piece(band, own_rows[member], columns[member])
        band = place_piece(band, got_next[member], next_cols[member])
        band = place_piece(band, got_far[member], far_cols[member])
    return band[None]


def solution(mesh):
    placed = (
        P(("sub", "fac"), None),
        P(("sub", "fac"), None),
        P(("sub", "fac"), None),
        P(("sub", "fac"), None),
        P(("sub", "fac")),
        P(("sub", "fac")),
        P("sub", None),
    )
    return jax.shard_map(
        shards, mesh=mesh, in_specs=placed, out_specs=P("fac", None, "sub", None), check_vma=False
    )
```

profile of v0, /device:TPU:0, one launch (start us, length us, event | category | flops | bytes accessed | tf_op | source)
XLA Modules:
  0.0 768.4 jit_solution(7867991064703560319)
XLA Ops:
  5.8 7.3 all-to-all-start.2
  18.7 3.4 all-to-all-done.2
  25.4 8.3 %all-to-all-done.1 = bf16[32,3,8,128]{3,2,1,0:T(8,128)(2,1)S(1)} async-done(((bf16[32,3,8,128]{3,2,1,0:T(8,128)(2,1)}), bf16[32,3,8,128]{3,2,1,0:T(8,128)(2,1)S(1)}, u32[]{:S(2)}, u32[]{:S(2)}) %all-to-all-start.1) | async-done | bytes 196640 | tf_op jit(solution)/shard_map/all_to_all | solution.py:136
  38.8 10.8 %all-to-all-done = bf16[32,3,8,256]{3,2,1,0:T(8,128)(2,1)S(1)} async-done(((bf16[32,3,8,256]{3,2,1,0:T(8,128)(2,1)}), bf16[32,3,8,256]{3,2,1,0:T(8,128)(2,1)S(1)}, u32[]{:S(2)}, u32[]{:S(2)}) %all-to-all-start) | async-done | bytes 393248 | tf_op jit(solution)/shard_map/all_to_all | solution.py:129
  50.2 218.1 %while.48 = (s32[]{:T(128)}, f32[512,256]{1,0:T(8,128)}, bf16[16,16,256]{2,1,0:T(8,128)(2,1)}, bf16[16,16,128]{2,1,0:T(8,128)(2,1)}, s32[16,16,4]{1,0,2:T(8,128)}, /*index=5*/s32[]{:T(128)}, s32[]{:T(128)}) while((s32[]{:T(128)}, f32[512,256]{1,0:T(8,128)}, bf16[16,16,256]{2,1,0:T(8,128)(2,1)}, ...), condition=%wide.region_9.10_spmd.clone.clone, body=%wide.region_8.9_spmd.clone.clone.sunk | while | flops 561235968 | bytes 18470300 | solution.py:92
  59.7 3.4 convolution_add_fusion.7
  73.3 3.4 convolution_add_fusion.7
  86.9 3.4 convolution_add_fusion.7
  100.6 3.4 convolution_add_fusion.7
  114.2 3.4 convolution_add_fusion.7
  127.8 3.4 convolution_add_fusion.7
  141.5 3.4 convolution_add_fusion.7
  155.1 3.4 convolution_add_fusion.7
  168.7 3.4 convolution_add_fusion.7
  182.3 3.4 convolution_add_fusion.7
  196.0 3.4 convolution_add_fusion.7
  209.6 3.4 convolution_add_fusion.7
  223.2 3.4 convolution_add_fusion.7
  236.9 3.4 convolution_add_fusion.7
  250.5 3.4 convolution_add_fusion.7
  264.1 3.4 convolution_add_fusion.7
  268.3 207.5 %while.49 = (s32[]{:T(128)}, f32[512,256]{1,0:T(8,128)}, bf16[16,16,256]{2,1,0:T(8,128)(2,1)S(1)}, bf16[16,16,128]{2,1,0:T(8,128)(2,1)}, s32[16,16,4]{1,0,2:T(8,128)}, /*index=5*/s32[]{:T(128)}, s32[]{:T(128)}) while((s32[]{:T(128)}, f32[512,256]{1,0:T(8,128)}, bf16[16,16,256]{2,1,0:T(8,128)(2,1)S(1)}, ...), condition=%wide.region_11.12_spmd.clone.clone, body=%wide.region_10.11_spmd.clone.clone.sunk | while | flops 561235968 | bytes 18470300 | solution.py:92
  277.1 3.4 convolution_add_fusion.8
  290.0 3.4 convolution_add_fusion.8
  303.0 3.4 convolution_add_fusion.8
  316.0 3.4 convolution_add_fusion.8
  328.9 3.4 convolution_add_fusion.8
  341.9 3.4 convolution_add_fusion.8
  354.9 3.4 convolution_add_fusion.8
  367.9 3.4 convolution_add_fusion.8
  380.8 3.4 convolution_add_fusion.8
  393.8 3.4 convolution_add_fusion.8
  406.8 3.4 convolution_add_fusion.8
  419.7 3.4 convolution_add_fusion.8
  432.7 3.4 convolution_add_fusion.8
  445.6 3.4 convolution_add_fusion.8
  458.6 3.4 convolution_add_fusion.8
  471.6 3.4 convolution_add_fusion.8
  475.8 185.3 %while.47 = (s32[]{:T(128)}, f32[512,256]{1,0:T(8,128)}, bf16[16,16,256]{2,1,0:T(8,128)(2,1)S(1)}, bf16[16,16,128]{2,1,0:T(8,128)(2,1)S(1)}, s32[16,16,4]{1,0,2:T(8,128)S(1)}, /*index=5*/s32[]{:T(128)}, s32[]{:T(128)}) while((s32[]{:T(128)}, f32[512,256]{1,0:T(8,128)}, bf16[16,16,256]{2,1,0:T(8,128)(2,1)S(1)}, ...), condition=%wide.region_7.8_spmd.clone.clone, body=%wide.region_6.7_spmd.clone.clone.sunk | while | flops 561235968 | bytes 18470300 | solution.py:92
  483.2 3.4 convolution_add_fusion.6
  494.8 3.4 convolution_add_fusion.6
  506.3 3.4 convolution_add_fusion.6
  517.9 3.4 convolution_add_fusion.6
  529.5 3.4 convolution_add_fusion.6
  541.1 3.4 convolution_add_fusion.6
  552.7 3.4 convolution_add_fusion.6
  564.3 3.4 convolution_add_fusion.6
  575.8 3.4 convolution_add_fusion.6
  587.4 3.4 convolution_add_fusion.6
  599.0 3.4 convolution_add_fusion.6
  610.6 3.4 convolution_add_fusion.6
  622.2 3.4 convolution_add_fusion.6
  633.8 3.4 convolution_add_fusion.6
  645.3 3.4 convolution_add_fusion.6
  656.9 3.4 convolution_add_fusion.6
  664.0 33.5 %while.46 = (s32[]{:T(128)}, f32[3,2,384,256]{3,2,1,0:T(8,128)S(1)}, s32[3,4]{1,0:T(4,128)S(1)}, f32[3,2,256,256]{3,2,1,0:T(8,128)}, s32[]{:T(128)}, /*index=5*/s32[4]{0:T(128)S(1)}, s32[]{:T(128)}) while((s32[]{:T(128)}, f32[3,2,384,256]{3,2,1,0:T(8,128)S(1)}, s32[3,4]{1,0:T(4,128)S(1)}, f32[3,2,256,256]{3,2,1,0:T(8,128)}, s32[]{:T(128)}, ...), condition=%wide.while_cond, body=%wide.while_body.sunk | while | flops 131101 | bytes 2621635 | solution.py:99
  664.7 3.3 and_reduce_fusion.2
  671.2 4.0 dynamic-update-slice.3
  675.9 3.3 and_reduce_fusion.2
  682.4 4.1 dynamic-update-slice.3
  687.2 3.3 and_reduce_fusion.2
  693.7 3.8 dynamic-update-slice.3
  708.1 13.9 %collective-permute-done = s32[3]{0:T(128)S(1)} collective-permute-done((s32[3]{0:T(128)S(1)}, s32[3]{0:T(128)S(1)}, u32[]{:S(2)}, u32[]{:S(2)}) %collective-permute-start) | collective-permute-done | bytes 44 | tf_op jit(solution)/shard_map/ppermute | solution.py:21
  734.4 4.4 broadcast_in_dim.550
  (994 shorter events, 514.4 us)
Async XLA Ops:
  0.0 36.4 %copy-start.9 = (s32[3]{0:T(128)S(1)}, s32[3]{0:T(128)}, u32[]{:S(2)}) copy-start(s32[3]{0:T(128)} %constant.1005.clone.1) | copy-start | bytes 40
  0.0 24.8 %copy-start.7 = (s32[3,2]{0,1:T(2,128)S(1)}, s32[3,2]{0,1:T(2,128)}, u32[]{:S(2)}) copy-start(s32[3,2]{0,1:T(2,128)} %param.19) | copy-start | bytes 76
  5.8 16.2 %all-to-all-start.2 = ((s32[32,3,8,4]{2,3,1,0:T(4,128)}), s32[32,3,8,4]{2,3,1,0:T(4,128)S(1)}, u32[]{:S(2)}, u32[]{:S(2)}) async-start(s32[32,3,8,4]{2,3,1,0:T(4,128)} %copy.32), calls=%async_computation.2 | async-start | bytes 393216 | tf_op jit(solution)/shard_map/all_to_all | solution.py:143
  22.0 11.6 %all-to-all-start.1 = ((bf16[32,3,8,128]{3,2,1,0:T(8,128)(2,1)}), bf16[32,3,8,128]{3,2,1,0:T(8,128)(2,1)S(1)}, u32[]{:S(2)}, u32[]{:S(2)}) async-start(bf16[32,3,8,128]{3,2,1,0:T(8,128)(2,1)} %bitcast.4), calls=%async_computation.1 | async-start | bytes 393216 | tf_op jit(solution)/shard_map/all_to_all | solution.py:136
  33.6 15.9 %all-to-all-start = ((bf16[32,3,8,256]{3,2,1,0:T(8,128)(2,1)}), bf16[32,3,8,256]{3,2,1,0:T(8,128)(2,1)S(1)}, u32[]{:S(2)}, u32[]{:S(2)}) async-start(bf16[32,3,8,256]{3,2,1,0:T(8,128)(2,1)} %bitcast.2), calls=%async_computation | async-start | bytes 786432 | tf_op jit(solution)/shard_map/all_to_all | solution.py:129
  58.6 1.0 copy-start.4
  72.3 1.0 copy-start.4
  85.9 1.0 copy-start.4
  99.5 1.0 copy-start.4
  113.2 1.0 copy-start.4
  126.8 1.0 copy-start.4
  140.4 1.0 copy-start.4
  154.0 1.0 copy-start.4
  167.7 1.0 copy-start.4
  181.3 1.0 copy-start.4
  194.9 1.0 copy-start.4
  208.6 1.0 copy-start.4
  222.2 1.0 copy-start.4
  235.8 1.0 copy-start.4
  249.5 1.0 copy-start.4
  263.1 1.0 copy-start.4
  276.0 1.0 copy-start.2
  289.0 1.0 copy-start.2
  293.4 0.8 copy-start.3
  302.0 1.0 copy-start.2
  314.9 1.0 copy-start.2
  319.4 0.8 copy-start.3
  327.9 1.0 copy-start.2
  340.9 1.0 copy-start.2
  345.3 0.8 copy-start.3
  353.8 1.0 copy-start.2
  366.8 1.0 copy-start.2
  379.8 1.0 copy-start.2
  384.2 0.8 copy-start.3
  392.7 1.0 copy-start.2
  397.2 0.8 copy-start.3
  405.7 1.0 copy-start.2
  418.7 1.0 copy-start.2
  431.6 1.0 copy-start.2
  444.6 1.0 copy-start.2
  457.6 1.0 copy-start.2
  470.6 1.0 copy-start.2
  482.1 1.0 copy-start
  493.7 1.0 copy-start
  505.3 1.0 copy-start
  516.9 1.0 copy-start
  528.5 1.0 copy-start
  540.1 1.0 copy-start
  551.6 1.0 copy-start
  563.2 1.0 copy-start
  574.8 1.0 copy-start
  586.4 1.0 copy-start
  598.0 1.0 copy-start
  609.5 1.0 copy-start
  621.1 1.0 copy-start
  632.7 1.0 copy-start
  644.3 1.0 copy-start
  655.9 1.0 copy-start
  661.1 2.9 copy-start.6
  697.5 1.7 copy-start.8
  698.6 42.5 %collective-permute-start.1 = (f32[3,2,128,256]{3,2,1,0:T(8,128)}, f32[3,2,128,256]{3,2,1,0:T(8,128)}, u32[]{:S(2)}, u32[]{:S(2)}) collective-permute-start(f32[3,2,128,256]{3,2,1,0:T(8,128)} %get-tuple-element.593), channel_id=1, source_target_pairs={{28,0},{0,4},{4,8},{8,12},{12,16},{16,20},{20,24},{24,28},{29,1},{... | collective-permute-start | bytes 2359304 | tf_op jit(solution)/shard_map/ppermute | solution.py:21
  699.2 22.9 %collective-permute-start = (s32[3]{0:T(128)S(1)}, s32[3]{0:T(128)S(1)}, u32[]{:S(2)}, u32[]{:S(2)}) collective-permute-start(s32[3]{0:T(128)S(1)} %copy-done.8), channel_id=1, source_target_pairs={{28,0},{0,4},{4,8},{8,12},{12,16},{16,20},{20,24},{24,28},{29,1},{... | collective-permute-start | bytes 44 | tf_op jit(solution)/shard_map/ppermute | solution.py:21
  701.6 22.5 %collective-permute-start.2 = (s32[3]{0:T(128)S(1)}, s32[3]{0:T(128)S(1)}, u32[]{:S(2)}, u32[]{:S(2)}) collective-permute-start(s32[3]{0:T(128)S(1)} %copy-done.8), channel_id=1, source_target_pairs={{24,0},{28,4},{0,8},{4,12},{8,16},{12,20},{16,24},{20,28},{25,1},{... | collective-permute-start | bytes 44 | tf_op jit(solution)/shard_map/ppermute | solution.py:21
  701.6 42.8 %collective-permute-start.3 = (f32[3,2,128,256]{3,2,1,0:T(8,128)S(1)}, f32[3,2,128,256]{3,2,1,0:T(8,128)}, u32[]{:S(2)}, u32[]{:S(2)}) collective-permute-start(f32[3,2,128,256]{3,2,1,0:T(8,128)S(1)} %get-tuple-element.592), channel_id=1, source_target_pairs={{24,0},{28,4},{0,8},{4,12},{8,16},{12,20},{16,24},{20,28},{25,1},{... | collective-permute-start | bytes 2359304 | tf_op jit(solution)/shard_map/ppermute | solution.py:21
  (43 other events, 34.5 us)
where the time goes:
time: 775 us; the launch traced here: 768 us
  other arithmetic  365 us (47%)
  local copies, waits for them, and re-layouts  167 us (22%)
  matrix products  162 us (21%)
  waiting for transfers between devices  36.4 us (5%)
  between operations  17 us (2%)
  starting transfers between devices  15.9 us (2%)
    dot_general x48, matrix products, step(): lax.dot_general(left, right, (((0,), (0,)), ((), ())), preferred_element_...  162 us
    convert_element_type x48, other arithmetic, step(): (jnp.transpose(scaled, (0, 2, 1))[..., None] * dense_v[:, :, None, :]).as...  136 us
    select_n x48, other arithmetic, dense_kernel(): result = jnp.where(offset == tap, weights[..., tap:tap + 1], result)  125 us
    while x240, local copies, waits for them, and re-layouts  71 us
    mul x96, other arithmetic, kaiser(): return (bessel_zero(kernel_beta * jnp.sqrt(inside)) - 1.0) * kernel_norm  30.9 us
    dynamic_slice x48, local copies, waits for them, and re-layouts, grid_rows(): lax.scan(step, jnp.zeros((2 * side, side), jnp.float32), pieces)  23.2 us
    convert_element_type x48, other arithmetic, step(): weight_block.astype(jnp.float32)[:, None, :]  22.1 us
    dynamic_update_slice x9, local copies, waits for them, and re-layouts, place_piece(): return lax.dynamic_update_slice(band, current + piece, (zero, zero, column))  20 us
  transfers between devices with their start and end apart: 7, of which 4 were waited for; matrix products, arithmetic and copies ran while one was open for 3% of the time, Pallas kernels for 0%

commit v1 on v0

v1 whole, which is shorter than its diff:
```python
import functools
import math

import jax
import jax.numpy as jnp
from jax import lax
from jax.experimental import pallas as pl
from jax.experimental.pallas import tpu as pltpu
from jax.sharding import PartitionSpec as P

SG = 256
GS = 8192
BAND = 128
LANES = 128
BATCH = 8
VMEM_LIMIT = 48 * 1024 * 1024

kernel_norm = 1.6e-07
SERIES = [kernel_norm * 81.0**k / math.factorial(k) ** 2 for k in range(1, 40)]

NT = (((1,), (1,)), ((), ()))
NN = (((1,), (0,)), ((), ()))


def iota(shape, axis):
    return lax.broadcasted_iota(jnp.int32, shape, axis)


def onehot(mask):
    return jnp.where(mask, 1.0, 0.0).astype(jnp.bfloat16)


def dot(a, b, dims=NN):
    return lax.dot_general(a, b, dims, preferred_element_type=jnp.float32)


def pack_kernel(capacity, dest_count, target, vis, weight, start, step, packet):
    rows = vis.shape[0]
    slots = packet.shape[0]
    goal = target[...]
    named = iota((dest_count, rows), 0) == goal
    ahead = onehot(iota((rows, rows), 0) < iota((rows, rows), 1))
    before = dot(onehot(named), ahead)
    rank = jnp.sum(jnp.where(named, before, 0.0), axis=0, keepdims=True)
    slot = goal * capacity + rank.astype(jnp.int32)
    place = onehot(iota((slots, rows), 0) == slot)
    lane = iota((rows, LANES), 1)
    begin, pace = start[...], step[...]
    value = jnp.where(lane < 3, begin[:, 0:1], begin[:, 1:2])
    value = jnp.where(lane < 6, value, pace[:, 0:1])
    value = jnp.where(lane < 8, value, pace[:, 1:2])
    piece = jnp.where(lane < 3, lane, lane - 3)
    piece = jnp.where(lane < 6, piece, lane - 6)
    piece = jnp.where(lane < 8, piece, lane - 8)
    piece = jnp.minimum(piece, 3) * 8
    value = jnp.right_shift(value, piece) & 255
    value = jnp.where(lane < 10, value, jnp.where(lane == 10, 1, 0))
    track = value.astype(jnp.float32).astype(jnp.bfloat16)
    packet[:, 0 : 2 * LANES] = dot(place, vis[...]).astype(jnp.bfloat16)
    packet[:, 2 * LANES : 3 * LANES] = dot(place, weight[...]).astype(jnp.bfloat16)
    packet[:, 3 * LANES : 4 * LANES] = dot(place, track).astype(jnp.bfloat16)


def sort_kernel(capacity, members, packet, scaled, position, counts):
    slots = packet.shape[0]
    part = slots // members
    track = packet[:, 3 * LANES : 4 * LANES]
    used = dot(onehot(iota((8, LANES), 1) == 10), track, NT)[0:1]
    slot = iota((1, slots), 1).astype(jnp.float32)
    group = jnp.floor((slot + 0.5) * (1.0 / capacity))
    cycle = jnp.floor((group + 0.5) * (1.0 / members))
    member = (group - cycle * members).astype(jnp.int32)
    ahead = onehot(iota((slots, slots), 0) < iota((slots, slots), 1))
    mine = (iota((8, slots), 0) == member) & (used > 0.5)
    before = dot(onehot(mine), ahead)
    rank = jnp.sum(jnp.where(mine, before, 0.0), axis=0, keepdims=True).astype(jnp.int32)
    goal = jnp.where(used > 0.5, member * part + rank, -1)
    place = onehot(iota((slots, slots), 0) == goal)
    for m in range(members):
        counts[m] = jnp.sum(jnp.where((member == m) & (used > 0.5), 1, 0))
    weight = dot(place, packet[:, 2 * LANES : 3 * LANES])
    scaled[:, 0:LANES] = dot(place, packet[:, 0:LANES]) * weight
    scaled[:, LANES : 2 * LANES] = dot(place, packet[:, LANES : 2 * LANES]) * weight
    line, chan = iota((LANES, LANES), 0), iota((LANES, LANES), 1)
    moved = dot(place, track).astype(jnp.bfloat16)
    for axis in range(2):
        mix = jnp.zeros((LANES, LANES), jnp.int32)
        for n in range(3):
            mix = jnp.where(line == 3 * axis + n, 256**n, mix)
        for n in range(2):
            mix = jnp.where(line == 6 + 2 * axis + n, chan * 256**n, mix)
        mix = mix.astype(jnp.float32).astype(jnp.bfloat16)
        position[:, axis * LANES : (axis + 1) * LANES] = dot(moved, mix).astype(jnp.int32)


def taps(place):
    shape = (place.shape[0], 8, LANES)
    spot = jnp.broadcast_to(place[:, None, :], shape)
    first = jnp.right_shift(spot, 10) - 3
    cell = first + ((iota(shape, 1) - first) & 7)
    offset = (cell * 1024 - spot).astype(jnp.float32) * (1.0 / 1024.0)
    inside = jnp.maximum(1.0 - offset * offset * 0.0625, 0.0)
    total = jnp.full(shape, SERIES[-1], jnp.float32)
    for term in SERIES[-2::-1]:
        total = total * inside + term
    return total * inside, cell


def halves(cell):
    block = jnp.right_shift(cell, 4)
    upper = (cell & 8) != 0
    low = jnp.where(upper, -1, block)
    high = jnp.where(upper, block, -1)
    return jnp.concatenate([low, high], axis=1).astype(jnp.float32).astype(jnp.bfloat16)


def twice(value):
    return jnp.concatenate([value, value], axis=1).astype(jnp.bfloat16)


def grid_kernel(member, scaled, position, counts, corner, own, near, far, left, right, total):
    total[...] = jnp.zeros_like(total)

    def batch(b, carry):
        rows = pl.ds(pl.multiple_of(b * BATCH, BATCH), BATCH)
        tap_u, cell_u = taps(position[rows, 0:LANES])
        tap_v, cell_v = taps(position[rows, LANES : 2 * LANES])
        block_u, block_v = halves(cell_u), halves(cell_v)
        right_tap = twice(tap_u)
        real = twice(scaled[rows, 0:LANES][:, None, :] * tap_v)
        imag = twice(scaled[rows, LANES : 2 * LANES][:, None, :] * tap_v)
        zero = jnp.zeros((16, LANES), jnp.bfloat16)
        for r in range(BATCH):
            cols = slice(r * LANES, (r + 1) * LANES)
            for k in range(SG // 16):
                here = block_u[r] == k
                right[k * 16 : (k + 1) * 16, cols] = jnp.where(here, right_tap[r], zero)
                here = block_v[r] == k
                left[k * 16 : (k + 1) * 16, cols] = jnp.where(here, real[r], zero)
                left[SG + k * 16 : SG + (k + 1) * 16, cols] = jnp.where(here, imag[r], zero)
        total[...] += dot(left[...], right[...], NT)
        return carry

    lax.fori_loop(0, (counts[member] + BATCH - 1) // BATCH, batch, 0)
    shift = corner[member, 0]
    for p in range(2):
        grid = total[p * SG : (p + 1) * SG, :]
        spread = jnp.concatenate([grid, jnp.zeros((BAND, SG), jnp.float32)], axis=0)
        spread = pltpu.roll(spread, shift, 0)
        own[p] = spread[0:BAND]
        near[p] = spread[BAND : 2 * BAND].astype(near.dtype)
        far[p] = spread[2 * BAND :].astype(far.dtype)


def place_kernel(count, columns, *refs):
    band = refs[-1]
    width = band.shape[-1]
    band[...] = jnp.zeros_like(band)
    for n, ref in enumerate(refs[:-1]):
        column = columns[n]
        base = jnp.minimum(lax.shift_right_logical(column, 7), (width - 3 * LANES) // LANES)
        piece = ref[0].astype(jnp.float32)
        piece = jnp.concatenate([piece, jnp.zeros((piece.shape[0], LANES), jnp.float32)], axis=1)
        piece = pltpu.roll(piece, column - base * LANES, 1)
        cols = pl.ds(pl.multiple_of(base * LANES, LANES), 3 * LANES)
        band[0, 0, :, cols] += piece


def params(**extra):
    return pltpu.CompilerParams(vmem_limit_bytes=VMEM_LIMIT, **extra)


def whole(count):
    return [pl.BlockSpec(memory_space=pltpu.VMEM)] * count


def shards(visibility, vis_weight, tap_start, tap_step, subgrid_id, w_plane, tile_intersection):
    sub_count = lax.axis_size("sub")
    fac_count = lax.axis_size("fac")
    rows, chans = vis_weight.shape
    members = tile_intersection.shape[0]
    dest_count = sub_count * fac_count * members
    capacity = max(2, (2 * rows + dest_count - 1) // dest_count)
    slots = dest_count * capacity
    part = slots // members
    smem = pl.BlockSpec(memory_space=pltpu.SMEM)

    columns = tile_intersection[:, 1]
    ring = lambda d: [((i - d) % sub_count, i) for i in range(sub_count)]
    next_cols = lax.ppermute(columns, "sub", ring(1))
    far_cols = lax.ppermute(columns, "sub", ring(2))

    target = (subgrid_id // members * fac_count + w_plane) * members + subgrid_id % members
    packet = pl.pallas_call(
        functools.partial(pack_kernel, capacity, dest_count),
        out_shape=jax.ShapeDtypeStruct((slots, 4 * LANES), jnp.bfloat16),
        in_specs=whole(5),
        out_specs=whole(1)[0],
        compiler_params=params(),
    )(target[None, :], visibility, vis_weight, tap_start, tap_step)
    packet = lax.all_to_all(
        packet.reshape(sub_count * fac_count, members * capacity, 4 * LANES),
        ("sub", "fac"),
        split_axis=0,
        concat_axis=0,
        tiled=True,
    ).reshape(slots, 4 * LANES)
    scaled, position, counts = pl.pallas_call(
        functools.partial(sort_kernel, capacity, members),
        out_shape=(
            jax.ShapeDtypeStruct((slots, 2 * LANES), jnp.float32),
            jax.ShapeDtypeStruct((slots, 2 * LANES), jnp.int32),
            jax.ShapeDtypeStruct((members,), jnp.int32),
        ),
        in_specs=whole(1),
        out_specs=(*whole(2), smem),
        compiler_params=params(),
    )(packet)

    owns, nears, fars = [], [], []
    for m in range(members):
        block = pl.BlockSpec((part, 2 * LANES), lambda i, m=m: (m, 0))
        piece = pl.BlockSpec((2, BAND, SG), lambda i: (0, 0, 0))
        own, near, far = pl.pallas_call(
            functools.partial(grid_kernel, m),
            grid=(1,),
            out_shape=(
                jax.ShapeDtypeStruct((2, BAND, SG), jnp.float32),
                jax.ShapeDtypeStruct((2, BAND, SG), jnp.bfloat16),
                jax.ShapeDtypeStruct((2, BAND, SG), jnp.bfloat16),
            ),
            in_specs=[block, block, smem, smem],
            out_specs=(piece, piece, piece),
            scratch_shapes=[
                pltpu.VMEM((2 * SG, BATCH * LANES), jnp.bfloat16),
                pltpu.VMEM((SG, BATCH * LANES), jnp.bfloat16),
                pltpu.VMEM((2 * SG, SG), jnp.float32),
            ],
            compiler_params=params(),
            cost_estimate=pl.CostEstimate(
                flops=2 * 2 * SG * SG * part * chans, bytes_accessed=2**20, transcendentals=0
            ),
        )(scaled, position, counts, tile_intersection)
        owns.append(own)
        nears.append(lax.ppermute(near, "sub", ring(1)))
        fars.append(lax.ppermute(far, "sub", ring(2)))

    places = jnp.concatenate([columns, next_cols, far_cols])
    high = 16
    cut = pl.BlockSpec((1, high, SG), lambda p, i: (p, i, 0))
    return pl.pallas_call(
        functools.partial(place_kernel, 3 * members),
        grid=(2, BAND // high),
        out_shape=jax.ShapeDtypeStruct((1, 2, BAND, GS), jnp.float32),
        in_specs=[smem] + [cut] * (3 * members),
        out_specs=pl.BlockSpec((1, 1, high, GS), lambda p, i: (0, p, i, 0)),
        compiler_params=params(),
    )(places, *owns, *nears, *fars)


def solution(mesh):
    placed = (
        P(("sub", "fac"), None),
        P(("sub", "fac"), None),
        P(("sub", "fac"), None),
        P(("sub", "fac"), None),
        P(("sub", "fac")),
        P(("sub", "fac")),
        P("sub", None),
    )
    return jax.shard_map(
        shards, mesh=mesh, in_specs=placed, out_specs=P("fac", None, "sub", None), check_vma=False
    )
```

time: 775 us -> 111 us (0.14)
  the two profiles are of different devices: /device:TPU:0 before, /device:TPU:7 now
where the time goes in v1:
time: 111 us; the launch traced here: 112 us
  Pallas kernels  56.3 us (51%)
  starting transfers between devices  28 us (25%)
  waiting for transfers between devices  22 us (20%)
  local copies, waits for them, and re-layouts  4.91 us (4%)
    pallas_call x3, Pallas kernels, shards(): pl.pallas_call(functools.partial(grid_kernel, m), grid=(1,), out_shape=(j...  44.5 us
    all_to_all x1, waiting for transfers between devices, shards(): lax.all_to_all(packet.reshape(sub_count * fac_count, members * capacity,...  15.9 us
    ppermute x3, starting transfers between devices, shards(): nears.append(lax.ppermute(near, 'sub', ring(1)))  14.3 us
    pallas_call x1, Pallas kernels, shards(): pl.pallas_call(functools.partial(place_kernel, 3 * members), grid=(2, BAN...  8.14 us
    all_to_all x1, starting transfers between devices, shards(): lax.all_to_all(packet.reshape(sub_count * fac_count, members * capacity,...  6.39 us
    ppermute x3, waiting for transfers between devices, shards(): fars.append(lax.ppermute(far, 'sub', ring(2)))  6.12 us
    ppermute x3, starting transfers between devices, shards(): fars.append(lax.ppermute(far, 'sub', ring(2)))  4.9 us
    unnamed x7, local copies, waits for them, and re-layouts  4.22 us
  transfers between devices with their start and end apart: 9, of which 4 were waited for; matrix products, arithmetic and copies ran while one was open for 1% of the time, Pallas kernels for 41%

profile of v1, /device:TPU:7, one launch (start us, length us, event | category | flops | bytes accessed | tf_op | source)
XLA Modules:
  0.0 112.2 jit_solution(14475184834664010131)
XLA Ops:
  0.0 0.7 fusion
  0.7 0.8 copy.8.start
  1.5 0.8 copy.9.step
  2.4 0.0 copy-start
  2.4 0.9 copy-done
  3.3 0.0 copy-start.1
  3.3 0.9 copy-done.1
  4.2 1.7 %shard_map.73 = bf16[768,512]{1,0:T(8,128)(2,1)} custom-call(s32[1,384]{1,0:T(1,128)S(1)} %broadcast_in_dim.3.target, bf16[384,256]{1,0:T(8,128)(2,1)S(1)} %copy-done, bf16[384,128]{1,0:T(8,128)(2,1)S(1)} %copy-done.1, s32[384,2]{1,0:T(8,128)S(1)} %copy.8.start, s32[384,2]{1,0:T(8,128)S(1)} %copy.9.step), custom_call_target="tpu_custom_call" | custom-call | tf_op jit(solution)/shard_map/pallas_call | solution.py:194
  5.9 6.4 %all-to-all-start = ((bf16[32,24,512]{2,1,0:T(8,128)(2,1)}), bf16[32,24,512]{2,1,0:T(8,128)(2,1)S(1)}, u32[]{:S(2)}, u32[]{:S(2)}) async-start(bf16[32,24,512]{2,1,0:T(8,128)(2,1)} %bitcast.1), calls=%async_computation | async-start | bytes 1572864 | tf_op jit(solution)/shard_map/all_to_all | solution.py:201
  12.3 0.7 slice_bitcast_fusion
  13.0 1.2 %collective-permute-start.1 = (s32[3]{0:T(128)S(1)}, s32[3]{0:T(128)S(1)}, u32[]{:S(2)}, u32[]{:S(2)}) collective-permute-start(s32[3]{0:T(128)S(1)} %slice_bitcast_fusion), channel_id=1, source_target_pairs={{24,0},{28,4},{0,8},{4,12},{8,16},{12,20},{16,24},{20,28},{25,1},{... | collective-permute-start | bytes 44 | tf_op jit(solution)/shard_map/ppermute | solution.py:191
  14.2 1.2 %collective-permute-start = (s32[3]{0:T(128)S(1)}, s32[3]{0:T(128)S(1)}, u32[]{:S(2)}, u32[]{:S(2)}) collective-permute-start(s32[3]{0:T(128)S(1)} %slice_bitcast_fusion), channel_id=1, source_target_pairs={{28,0},{0,4},{4,8},{8,12},{12,16},{16,20},{20,24},{24,28},{29,1},{... | collective-permute-start | bytes 44 | tf_op jit(solution)/shard_map/ppermute | solution.py:190
  15.4 0.8 copy.10.corner
  16.1 15.9 %all-to-all-done = bf16[32,24,512]{2,1,0:T(8,128)(2,1)S(1)} async-done(((bf16[32,24,512]{2,1,0:T(8,128)(2,1)}), bf16[32,24,512]{2,1,0:T(8,128)(2,1)S(1)}, u32[]{:S(2)}, u32[]{:S(2)}) %all-to-all-start) | async-done | bytes 786464 | tf_op jit(solution)/shard_map/all_to_all | solution.py:201
  32.1 1.9 %shard_map.74 = (f32[768,256]{1,0:T(8,128)S(1)}, s32[768,256]{1,0:T(8,128)S(1)}, s32[3]{0:T(128)S(1)}) custom-call(bf16[768,512]{1,0:T(8,128)(2,1)S(1)} %bitcast.4), custom_call_target="tpu_custom_call" | custom-call | tf_op jit(solution)/shard_map/pallas_call | solution.py:208
  34.0 14.6 %shard_map.77 = (f32[2,128,256]{2,1,0:T(8,128)S(1)}, bf16[2,128,256]{2,1,0:T(8,128)(2,1)S(1)}, bf16[2,128,256]{2,1,0:T(8,128)(2,1)S(1)}) custom-call(f32[768,256]{1,0:T(8,128)S(1)} %get-tuple-element.17.scaled, s32[768,256]{1,0:T(8,128)S(1)} %get-tuple-element.18.position, s32[3]{0:T(128)S(1)} %get-tuple-element.19.counts, s32[3,2]{1,0:T(4,128)S(1)} %copy.10.corner), custom_call_target="tpu_custom_call" | custom-call | flops 8589934592 | bytes 1048576 | tf_op jit(solution)/shard_map/pallas_call | solution.py:224
  48.6 13.8 %shard_map.76 = (f32[2,128,256]{2,1,0:T(8,128)S(1)}, bf16[2,128,256]{2,1,0:T(8,128)(2,1)S(1)}, bf16[2,128,256]{2,1,0:T(8,128)(2,1)S(1)}) custom-call(f32[768,256]{1,0:T(8,128)S(1)} %get-tuple-element.17.scaled, s32[768,256]{1,0:T(8,128)S(1)} %get-tuple-element.18.position, s32[3]{0:T(128)S(1)} %get-tuple-element.19.counts, s32[3,2]{1,0:T(4,128)S(1)} %copy.10.corner), custom_call_target="tpu_custom_call" | custom-call | flops 8589934592 | bytes 1048576 | tf_op jit(solution)/shard_map/pallas_call | solution.py:224
  62.3 14.2 %collective-permute-start.4 = (bf16[2,128,256]{2,1,0:T(8,128)(2,1)S(1)}, bf16[2,128,256]{2,1,0:T(8,128)(2,1)S(1)}, u32[]{:S(2)}, u32[]{:S(2)}) collective-permute-start(bf16[2,128,256]{2,1,0:T(8,128)(2,1)S(1)} %get-tuple-element.25), channel_id=1, source_target_pairs={{28,0},{0,4},{4,8},{8,12},{12,16},{16,20},{20,24},{24,28},{29,1},{... | collective-permute-start | bytes 393224 | tf_op jit(solution)/shard_map/ppermute | solution.py:245
  76.6 16.2 %shard_map.75 = (f32[2,128,256]{2,1,0:T(8,128)S(1)}, bf16[2,128,256]{2,1,0:T(8,128)(2,1)S(1)}, bf16[2,128,256]{2,1,0:T(8,128)(2,1)S(1)}) custom-call(f32[768,256]{1,0:T(8,128)S(1)} %get-tuple-element.17.scaled, s32[768,256]{1,0:T(8,128)S(1)} %get-tuple-element.18.position, s32[3]{0:T(128)S(1)} %get-tuple-element.19.counts, s32[3,2]{1,0:T(4,128)S(1)} %copy.10.corner), custom_call_target="tpu_custom_call" | custom-call | flops 8589934592 | bytes 1048576 | tf_op jit(solution)/shard_map/pallas_call | solution.py:224
  92.7 0.1 collective-permute-start.7
  92.8 0.1 collective-permute-start.3
  92.9 0.0 collective-permute-done.1
  92.9 0.1 collective-permute-start.6
  93.0 0.0 collective-permute-done
  93.0 0.1 collective-permute-start.2
  93.0 0.0 collective-permute-done.4.refs_5_
  93.0 4.8 %collective-permute-start.5 = (bf16[2,128,256]{2,1,0:T(8,128)(2,1)S(1)}, bf16[2,128,256]{2,1,0:T(8,128)(2,1)S(1)}, u32[]{:S(2)}, u32[]{:S(2)}) collective-permute-start(bf16[2,128,256]{2,1,0:T(8,128)(2,1)S(1)} %get-tuple-element.26), channel_id=1, source_target_pairs={{24,0},{28,4},{0,8},{4,12},{8,16},{12,20},{16,24},{20,28},{25,1},{... | collective-permute-start | bytes 393224 | tf_op jit(solution)/shard_map/ppermute | solution.py:246
  97.8 0.1 pad_add_fusion.columns
  97.9 0.5 collective-permute-done.7.refs_8_
  98.4 0.0 collective-permute-done.3.refs_4_
  98.4 2.8 %collective-permute-done.6.refs_7_ = bf16[2,128,256]{2,1,0:T(8,128)(2,1)S(1)} collective-permute-done((bf16[2,128,256]{2,1,0:T(8,128)(2,1)S(1)}, bf16[2,128,256]{2,1,0:T(8,128)(2,1)S(1)}, u32[]{:S(2)}, u32[]{:S(2)}) %collective-permute-start.6) | collective-permute-done | bytes 131104 | tf_op jit(solution)/shard_map/ppermute | solution.py:246
  101.2 0.0 collective-permute-done.2.refs_3_
  101.2 2.8 %collective-permute-done.5.refs_6_ = bf16[2,128,256]{2,1,0:T(8,128)(2,1)S(1)} collective-permute-done((bf16[2,128,256]{2,1,0:T(8,128)(2,1)S(1)}, bf16[2,128,256]{2,1,0:T(8,128)(2,1)S(1)}, u32[]{:S(2)}, u32[]{:S(2)}) %collective-permute-start.5) | collective-permute-done | bytes 131104 | tf_op jit(solution)/shard_map/ppermute | solution.py:246
  104.0 8.1 %shard_map.78 = f32[1,2,128,8192]{3,2,1,0:T(8,128)} custom-call(s32[9]{0:T(128)S(1)} %pad_add_fusion.columns, f32[2,128,256]{2,1,0:T(8,128)S(1)} %get-tuple-element.20.refs_0_, f32[2,128,256]{2,1,0:T(8,128)S(1)} %get-tuple-element.21.refs_1_, f32[2,128,256]{2,1,0:T(8,128)S(1)} %get-tuple-element.22.refs_2_, ...), custom_call_target="tpu_custom_call" | custom-call | tf_op jit(solution)/shard_map/pallas_call | solution.py:251
  (1 shorter events, 0.0 us)
Async XLA Ops:
  2.4 0.9 copy-start
  3.3 0.9 copy-start.1
  5.9 26.1 %all-to-all-start = ((bf16[32,24,512]{2,1,0:T(8,128)(2,1)}), bf16[32,24,512]{2,1,0:T(8,128)(2,1)S(1)}, u32[]{:S(2)}, u32[]{:S(2)}) async-start(bf16[32,24,512]{2,1,0:T(8,128)(2,1)} %bitcast.1), calls=%async_computation | async-start | bytes 1572864 | tf_op jit(solution)/shard_map/all_to_all | solution.py:201
  13.0 79.9 %collective-permute-start.1 = (s32[3]{0:T(128)S(1)}, s32[3]{0:T(128)S(1)}, u32[]{:S(2)}, u32[]{:S(2)}) collective-permute-start(s32[3]{0:T(128)S(1)} %slice_bitcast_fusion), channel_id=1, source_target_pairs={{24,0},{28,4},{0,8},{4,12},{8,16},{12,20},{16,24},{20,28},{25,1},{... | collective-permute-start | bytes 44 | tf_op jit(solution)/shard_map/ppermute | solution.py:191
  14.2 78.8 %collective-permute-start = (s32[3]{0:T(128)S(1)}, s32[3]{0:T(128)S(1)}, u32[]{:S(2)}, u32[]{:S(2)}) collective-permute-start(s32[3]{0:T(128)S(1)} %slice_bitcast_fusion), channel_id=1, source_target_pairs={{28,0},{0,4},{4,8},{8,12},{12,16},{16,20},{20,24},{24,28},{29,1},{... | collective-permute-start | bytes 44 | tf_op jit(solution)/shard_map/ppermute | solution.py:190
  62.3 30.7 %collective-permute-start.4 = (bf16[2,128,256]{2,1,0:T(8,128)(2,1)S(1)}, bf16[2,128,256]{2,1,0:T(8,128)(2,1)S(1)}, u32[]{:S(2)}, u32[]{:S(2)}) collective-permute-start(bf16[2,128,256]{2,1,0:T(8,128)(2,1)S(1)} %get-tuple-element.25), channel_id=1, source_target_pairs={{28,0},{0,4},{4,8},{8,12},{12,16},{16,20},{20,24},{24,28},{29,1},{... | collective-permute-start | bytes 393224 | tf_op jit(solution)/shard_map/ppermute | solution.py:245
  92.7 5.7 %collective-permute-start.7 = (bf16[2,128,256]{2,1,0:T(8,128)(2,1)S(1)}, bf16[2,128,256]{2,1,0:T(8,128)(2,1)S(1)}, u32[]{:S(2)}, u32[]{:S(2)}) collective-permute-start(bf16[2,128,256]{2,1,0:T(8,128)(2,1)S(1)} %get-tuple-element.28), channel_id=1, source_target_pairs={{24,0},{28,4},{0,8},{4,12},{8,16},{12,20},{16,24},{20,28},{25,1},{... | collective-permute-start | bytes 393224 | tf_op jit(solution)/shard_map/ppermute | solution.py:246
  92.8 5.6 %collective-permute-start.3 = (bf16[2,128,256]{2,1,0:T(8,128)(2,1)S(1)}, bf16[2,128,256]{2,1,0:T(8,128)(2,1)S(1)}, u32[]{:S(2)}, u32[]{:S(2)}) collective-permute-start(bf16[2,128,256]{2,1,0:T(8,128)(2,1)S(1)} %get-tuple-element.24), channel_id=1, source_target_pairs={{28,0},{0,4},{4,8},{8,12},{12,16},{16,20},{20,24},{24,28},{29,1},{... | collective-permute-start | bytes 393224 | tf_op jit(solution)/shard_map/ppermute | solution.py:245
  92.9 8.3 %collective-permute-start.6 = (bf16[2,128,256]{2,1,0:T(8,128)(2,1)S(1)}, bf16[2,128,256]{2,1,0:T(8,128)(2,1)S(1)}, u32[]{:S(2)}, u32[]{:S(2)}) collective-permute-start(bf16[2,128,256]{2,1,0:T(8,128)(2,1)S(1)} %get-tuple-element.27), channel_id=1, source_target_pairs={{24,0},{28,4},{0,8},{4,12},{8,16},{12,20},{16,24},{20,28},{25,1},{... | collective-permute-start | bytes 393224 | tf_op jit(solution)/shard_map/ppermute | solution.py:246
  93.0 8.3 %collective-permute-start.2 = (bf16[2,128,256]{2,1,0:T(8,128)(2,1)S(1)}, bf16[2,128,256]{2,1,0:T(8,128)(2,1)S(1)}, u32[]{:S(2)}, u32[]{:S(2)}) collective-permute-start(bf16[2,128,256]{2,1,0:T(8,128)(2,1)S(1)} %get-tuple-element.23), channel_id=1, source_target_pairs={{28,0},{0,4},{4,8},{8,12},{12,16},{16,20},{20,24},{24,28},{29,1},{... | collective-permute-start | bytes 393224 | tf_op jit(solution)/shard_map/ppermute | solution.py:245
  93.0 11.0 %collective-permute-start.5 = (bf16[2,128,256]{2,1,0:T(8,128)(2,1)S(1)}, bf16[2,128,256]{2,1,0:T(8,128)(2,1)S(1)}, u32[]{:S(2)}, u32[]{:S(2)}) collective-permute-start(bf16[2,128,256]{2,1,0:T(8,128)(2,1)S(1)} %get-tuple-element.26), channel_id=1, source_target_pairs={{24,0},{28,4},{0,8},{4,12},{8,16},{12,20},{16,24},{20,28},{25,1},{... | collective-permute-start | bytes 393224 | tf_op jit(solution)/shard_map/ppermute | solution.py:246
